TPU v7x, 32 devices: a whole 2x2x4 slice. The times are simulated.
32 devices in a mesh: dom: 16 (over z, y, core), sub: 2 (over x).
Axes of the slice: x: 2, y: 2, z: 4, core: 2. Of those that a mesh axis runs over, the one named last changes fastest.
Arguments:
- modal_state: float32 [35, 9, 4096], P(None, None, ('dom', 'sub')), may hold values from -6 to 6
- star_matrices: float32 [3, 9, 9, 4096], P(None, None, None, ('dom', 'sub')), may hold values from -2 to 2
- face_normals: float32 [3, 4, 4096], P(None, None, ('dom', 'sub')), may hold values from -4 to 4
- wave_speed: float32 [4096], P(('dom', 'sub')), may hold values from 1 to 3
- inverse_jacobian: float32 [4096], P(('dom', 'sub')), may hold values from 0.02 to 0.2
- stiffness: float32 [3, 35, 35], replicated, may hold values from -1 to 1
- lift_minus: float32 [4, 35, 35], replicated, may hold values from -1 to 1
- lift_plus: float32 [4, 35, 35], replicated, may hold values from -1 to 1
- cluster: int32 [4096], P(('dom', 'sub')), may hold values from 0 to 1, as said below
- face_source: int32 [4, 4096], P(None, ('dom', 'sub')), may hold values from 0 to 167, as said below
- send_rows: int32 [32, 2, 5, 2, 4], P(('dom', 'sub')), may hold values from 0 to 127
- send_counts: int32 [32, 2, 5, 2], P(('dom', 'sub')), may hold values from 0 to 4, as said below
Outputs:
- new_state: float32 [35, 9, 4096], P(None, None, ('dom', 'sub'))
Inputs may be any that keep to these rules, and one draw needn't show every extreme that they name: At most 16 elements of one device have cluster 0, and some device has exactly 16. `face_source`: values below 128 name a local element; a larger value names a row of the receive pool of the element's own cluster list. `send_counts`: zero for a device's own slot (offset 2, its own sub index) and for targets beyond the ends of dom; some count equals 4.
All inputs are finite; a program needn't handle non-finite values.
Results may differ from a plain program's by a relative error of at most 0.0003.
Values sent between devices are 32-bit elements; how exact they have to be, the bound alone decides.
A program may use at most 64 MiB of HBM per device.

v0:
```python
import functools
import math

import jax
import jax.numpy as jnp
from jax import lax
from jax.experimental import pallas as pl
from jax.experimental.pallas import tpu as pltpu
from jax.sharding import PartitionSpec as P

DEGREE = 4
HALF = 0.5
MESH = pl.DeviceIdType.MESH
f32, bf16 = jnp.float32, jnp.bfloat16


def up(value, step):
    return (value + step - 1) // step * step


def halves(value):
    high = value.astype(bf16).astype(f32)
    return high, value - high


def matmul(left, right, dims=((1,), (0,))):
    return lax.dot_general(
        left.astype(bf16), right.astype(bf16), (dims, ((), ())), preferred_element_type=f32
    )


def pick_coefficient(step, values):
    result = jnp.float32(values[-1])
    for index in range(len(values) - 1):
        result = jnp.where(step == index, jnp.float32(values[index]), result)
    return result


def kernel(
    n_dom,
    n_sub,
    modal,
    star,
    normals,
    speed,
    jacobian,
    stiffness,
    lift_minus,
    lift_plus,
    cluster,
    face_source,
    send_rows,
    send_counts,
    out,
    grad_mat,
    back_mat,
    lift_mat,
    cur,
    early,
    late,
    mid,
    value,
    coarse,
    zed,
    dee,
    faces,
    slot_rows,
    near_hot,
    far_hot,
    send_buf,
    recv_buf,
    send_sem,
    recv_sem,
):
    quants, basis, elems = modal.shape
    rows = cur.shape[0]
    offsets = send_counts.shape[3]
    slots = send_rows.shape[3]
    span = (offsets - 1) // 2
    blocks = offsets * n_sub
    pool_rows = blocks * 2 * slots
    my_dom, my_sub = lax.axis_index("dom"), lax.axis_index("sub")

    def lane(q):
        return slice(q * elems, (q + 1) * elems)

    def partners(step_sign, action):
        for o in range(offsets):
            other = my_dom + step_sign * (o - span)
            for t in range(n_sub):
                good = (other >= 0) & (other < n_dom)
                if o == span:
                    good = my_sub != t

                @pl.when(good)
                def _():
                    action(o, t, other)

    barrier = pltpu.get_barrier_semaphore()
    recv_buf[...] = jnp.zeros_like(recv_buf)

    def greet(o, t, other):
        pl.semaphore_signal(barrier, inc=1, device_id=(other, t), device_id_type=MESH)

    partners(1, greet)

    for scratch in (grad_mat, back_mat, lift_mat, cur):
        scratch[...] = jnp.zeros_like(scratch)

    def place(ref, row, column, matrix):
        high, low = halves(matrix)
        for index, part in enumerate((high, low, high)):
            start = column + index * rows
            ref[row : row + basis, start : start + basis] = part

    for d in range(3):
        place(grad_mat, d * rows, 0, -stiffness[d])
        place(back_mat, d * rows, 0, stiffness[d].T)
    for f in range(4):
        own, far = 0.5 * lift_minus[:, f, :], 0.5 * lift_plus[:, f, :]
        place(lift_mat.at[f], 0, 0, own)
        place(lift_mat.at[f], 0, 3 * rows, far)
        place(lift_mat.at[f], rows, 0, own)
        place(lift_mat.at[f], rows, 3 * rows, -far)

    for q in range(quants):
        cur[:basis, lane(q)] = modal[q]

    coarse_row = cluster[...]
    is_fine = coarse_row == 0
    near_iota = lax.broadcasted_iota(jnp.int32, (elems, elems), 0)
    far_iota = lax.broadcasted_iota(jnp.int32, (pool_rows, elems), 0)
    for f in range(4):
        source = face_source[f : f + 1, :]
        near_hot[:, lane(f)] = jnp.where(near_iota == source, 1.0, 0.0)
        index = source - elems
        block = index // slots
        index = jnp.where(index >= 0, block * (2 * slots) + (index - block * slots) + slots * coarse_row, -1)
        far_hot[:, lane(f)] = jnp.where(far_iota == index, 1.0, 0.0)
    slot_iota = lax.broadcasted_iota(jnp.int32, (slots, elems), 0)
    for o in range(offsets):
        for t in range(n_sub):
            for part in range(2):
                row = ((o * n_sub + t) * 2 + part) * slots
                ids = jnp.broadcast_to(send_rows[0, part, t, :, o : o + 1], (slots, elems))
                live = jnp.broadcast_to(send_counts[0, part, t : t + 1, o : o + 1], (slots, elems))
                slot_rows[row : row + slots, :] = jnp.where(slot_iota < live, ids, -1)
    send_iota = lax.broadcasted_iota(jnp.int32, (pool_rows, elems), 1)
    send_hot = jnp.where(send_iota == slot_rows[...], 1.0, 0.0)
    slot_list = (lax.broadcasted_iota(jnp.int32, (pool_rows, elems), 0) // slots) % 2

    def stacked(source):
        high, low = halves(source)
        return jnp.concatenate([high, high, low], axis=0).astype(bf16)

    def tall(source):
        return jnp.concatenate([source[:, lane(q)] for q in range(quants)], axis=0)

    def mix(finish):
        group = 3
        for first in range(0, quants, group):
            wanted = range(first, min(first + group, quants))
            total = {q: None for q in wanted}
            for d in range(3):
                for p in range(quants):
                    block = zed[d * rows : (d + 1) * rows, lane(p)]
                    for q in wanted:
                        term = block * star[p, q, d : d + 1, :]
                        total[q] = term if total[q] is None else total[q] + term
            for q in wanted:
                finish(q, total[q])

    def expand(sums):
        def step(index, carry):
            zed[...] = matmul(grad_mat[...], stacked(cur[...]))
            scales = [pick_coefficient(index, values) for _, values in sums]

            def finish(q, total):
                cur[:, lane(q)] = total
                for (ref, _), scale in zip(sums, scales):
                    ref[:, lane(q)] = ref[:, lane(q)] + scale * total

            mix(finish)
            return carry

        lax.fori_loop(0, DEGREE, step, 0)

    def weights(low, high):
        return [
            (high ** (k + 1) - low ** (k + 1)) / float(math.factorial(k + 1))
            for k in range(1, DEGREE + 1)
        ]

    def copy(turn, o, t, other):
        block = o * n_sub + my_sub
        return pltpu.make_async_remote_copy(
            src_ref=send_buf.at[turn, o * n_sub + t],
            dst_ref=recv_buf.at[turn, block],
            send_sem=send_sem.at[turn, o * n_sub + t],
            recv_sem=recv_sem.at[turn, block],
            device_id=(other, t),
            device_id_type=MESH,
        )

    def arrival(turn, o, t, other):
        block = o * n_sub + t
        return pltpu.make_async_remote_copy(
            src_ref=send_buf.at[turn, block],
            dst_ref=recv_buf.at[turn, block],
            send_sem=send_sem.at[turn, block],
            recv_sem=recv_sem.at[turn, block],
            device_id=(other, t),
            device_id_type=MESH,
        )

    def send(turn, picked):
        width = picked.shape[1]
        for block in range(blocks):
            first = block * 2 * slots
            send_buf[turn, block, :, :width] = picked[first : first + 2 * slots, :]
        if turn == 0:
            below = jnp.minimum(my_dom, span)
            above = jnp.minimum(n_dom - 1 - my_dom, span)
            pl.semaphore_wait(barrier, (below + above + 1) * n_sub - 1)
        partners(1, lambda o, t, other: copy(turn, o, t, other).start())

    def pick(hot, source):
        high, low = halves(source)
        return matmul(hot, high, ((1,), (1,))) + matmul(hot, low, ((1,), (1,)))

    def update(turn, integral, near_left, near_right, finish):
        high, low = halves(near_left)
        faces[...] = matmul(jnp.concatenate([high, low], axis=0), near_right)
        own = stacked(integral)
        zed[...] = matmul(back_mat[...], own)
        partners(-1, lambda o, t, other: arrival(turn, o, t, other).wait_recv())
        pool = recv_buf[turn].reshape(pool_rows, recv_buf.shape[3])
        high, low = halves(pool.T)
        wide = quants * rows
        faces[...] += matmul(jnp.concatenate([high[:wide], low[:wide]], axis=0), far_hot[...])
        for f in range(4):
            parts = [
                jnp.concatenate(
                    [
                        faces[base + q * rows : base + (q + 1) * rows, lane(f)]
                        for q in range(quants)
                    ],
                    axis=1,
                )
                for base in (0, wide)
            ]
            theirs = jnp.concatenate([parts[0], parts[0], parts[1]], axis=0).astype(bf16)
            lifted = matmul(lift_mat[f, :, : 3 * rows], own) + matmul(
                lift_mat[f, :, 3 * rows :], theirs
            )
            for q in range(quants):
                block = lifted[:rows, lane(q)]
                for d in range(3):
                    zed[d * rows : (d + 1) * rows, lane(q)] -= (
                        normals[d, f : f + 1, :] * block
                    )
                other = lifted[rows:, lane(q)]
                dee[:, lane(q)] = other if f == 0 else dee[:, lane(q)] + other
        mix(lambda q, total: finish(q, total - speed[...] * dee[:, lane(q)]))

    early[...] = HALF * cur[...]
    late[...] = HALF * cur[...]
    mid[...] = cur[...]
    expand([(early, weights(0.0, HALF)), (late, weights(HALF, 2 * HALF))])
    early_tall = tall(early[...])
    send(0, pick(send_hot, early_tall))

    def keep_mid(q, total):
        result = mid[:, lane(q)] + jacobian[...] * total
        cur[:, lane(q)] = result
        value[:, lane(q)] = HALF * result
        mid[:, lane(q)] = jnp.where(is_fine, result, mid[:, lane(q)])

    update(0, early[...], early_tall, near_hot[...], keep_mid)
    expand([(value, weights(0.0, HALF))])
    for q in range(quants):
        fine = jnp.where(is_fine, value[:, lane(q)], late[:, lane(q)])
        value[:, lane(q)] = fine
        coarse[:, lane(q)] = early[:, lane(q)] + fine
    both = jnp.concatenate([tall(value[...]), tall(coarse[...])], axis=1)
    both_hot = jnp.concatenate(
        [jnp.where(slot_list == 0, send_hot, 0.0), jnp.where(slot_list == 1, send_hot, 0.0)], axis=1
    )
    send(1, pick(both_hot, both))
    fine_lanes = jnp.concatenate([is_fine.astype(f32)] * 4, axis=1)
    near_both = jnp.concatenate(
        [near_hot[...] * fine_lanes, near_hot[...] * (1.0 - fine_lanes)], axis=0
    )
    for q in range(quants):
        cur[:, lane(q)] = jnp.where(is_fine, value[:, lane(q)], coarse[:, lane(q)])

    def keep_end(q, total):
        out[q] = (mid[:, lane(q)] + jacobian[...] * total)[:basis]

    update(1, cur[...], both, near_both, keep_end)
    for turn in range(2):
        partners(1, lambda o, t, other: copy(turn, o, t, other).wait_send())


def per_device(n_dom, n_sub, modal_state, star_matrices, face_normals, wave_speed, inverse_jacobian,
               stiffness, lift_minus, lift_plus, cluster, face_source, send_rows, send_counts):
    basis, quants, elems = modal_state.shape
    rows = up(basis, 8)
    wide = quants * elems
    blocks = send_counts.shape[2] * n_sub
    slots = send_rows.shape[4]
    pool_rows = blocks * 2 * slots
    message = (2, blocks, 2 * slots, up(quants * rows, 128))
    state = pltpu.VMEM((rows, wide), f32)
    result = pl.pallas_call(
        functools.partial(kernel, n_dom, n_sub),
        out_shape=jax.ShapeDtypeStruct((quants, basis, elems), f32),
        in_specs=[pl.BlockSpec(memory_space=pltpu.VMEM)] * 12,
        out_specs=pl.BlockSpec(memory_space=pltpu.VMEM),
        scratch_shapes=[
            pltpu.VMEM((3 * rows, 3 * rows), f32),
            pltpu.VMEM((3 * rows, 3 * rows), f32),
            pltpu.VMEM((4, 2 * rows, 6 * rows), f32),
            state,
            state,
            state,
            state,
            state,
            state,
            pltpu.VMEM((3 * rows, wide), f32),
            state,
            pltpu.VMEM((2 * quants * rows, 4 * elems), f32),
            pltpu.VMEM((pool_rows, elems), jnp.int32),
            pltpu.VMEM((elems, 4 * elems), f32),
            pltpu.VMEM((pool_rows, 4 * elems), f32),
            pltpu.VMEM(message, f32),
            pltpu.VMEM(message, f32),
            pltpu.SemaphoreType.DMA((2, blocks)),
            pltpu.SemaphoreType.DMA((2, blocks)),
        ],
        compiler_params=pltpu.CompilerParams(
            collective_id=0, has_side_effects=True, vmem_limit_bytes=32 * 1024 * 1024
        ),
    )(
        modal_state.transpose(1, 0, 2),
        star_matrices.transpose(1, 2, 0, 3),
        face_normals,
        wave_speed[None],
        inverse_jacobian[None],
        stiffness,
        lift_minus.transpose(1, 0, 2),
        lift_plus.transpose(1, 0, 2),
        cluster[None],
        face_source,
        send_rows.transpose(0, 1, 3, 4, 2),
        send_counts.transpose(0, 1, 3, 2),
    )
    return result.transpose(1, 0, 2)


def solution(mesh):
    placed = (
        P(None, None, ("dom", "sub")),
        P(None, None, None, ("dom", "sub")),
        P(None, None, ("dom", "sub")),
        P(("dom", "sub")),
        P(("dom", "sub")),
        P(),
        P(),
        P(),
        P(("dom", "sub")),
        P(None, ("dom", "sub")),
        P(("dom", "sub"), None, None, None, None),
        P(("dom", "sub"), None, None, None),
    )
    return jax.shard_map(
        functools.partial(per_device, mesh.shape["dom"], mesh.shape["sub"]),
        mesh=mesh,
        in_specs=placed,
        out_specs=P(None, None, ("dom", "sub")),
        check_vma=False,
    )
```

profile of v0, /device:TPU:0, one launch (start us, length us, event | category | flops | bytes accessed | tf_op | source)
XLA Modules:
  0.0 25.9 jit_solution(14918953919368725189)
XLA Ops:
  0.0 0.0 copy-start.7
  0.0 0.0 copy-start.5
  0.0 0.0 copy-start.6
  0.0 0.0 copy-start.9
  0.0 0.0 copy-start.10
  0.0 0.7 %copy-done.7 = s32[4,128]{1,0:T(4,128)S(1)} copy-done((s32[4,128]{1,0:T(4,128)S(1)}, s32[4,128]{1,0:T(4,128)}, u32[]{:S(2)}) %copy-start.7) | copy-done | bytes 2072
  0.7 0.0 copy-done.5
  0.7 0.0 copy-done.6
  0.7 0.0 copy-done.9
  0.7 0.0 copy-done.10
  0.7 0.0 copy-start
  0.7 0.9 %copy-done = f32[35,9,128]{2,0,1:T(8,128)S(1)} copy-done((f32[35,9,128]{2,0,1:T(8,128)S(1)}, f32[35,9,128]{2,0,1:T(8,128)}, u32[]{:S(2)}) %copy-start) | copy-done | bytes 161304
  1.7 0.0 copy-start.1
  1.7 0.9 %copy-done.1 = f32[3,9,9,128]{3,0,2,1:T(4,128)S(1)} copy-done((f32[3,9,9,128]{3,0,2,1:T(4,128)S(1)}, f32[3,9,9,128]{3,0,2,1:T(4,128)}, u32[]{:S(2)}) %copy-start.1) | copy-done | bytes 124440
  2.6 0.0 copy-start.2
  2.6 0.9 %copy-done.2 = f32[4,35,35]{2,0,1:T(4,128)S(1)} copy-done((f32[4,35,35]{2,0,1:T(4,128)S(1)}, f32[4,35,35]{2,0,1:T(4,128)}, u32[]{:S(2)}) %copy-start.2) | copy-done | bytes 19624
  3.5 0.0 copy-start.3
  3.5 0.9 %copy-done.3 = f32[4,35,35]{2,0,1:T(4,128)S(1)} copy-done((f32[4,35,35]{2,0,1:T(4,128)S(1)}, f32[4,35,35]{2,0,1:T(4,128)}, u32[]{:S(2)}) %copy-start.3) | copy-done | bytes 19624
  4.3 0.0 copy-start.4
  4.3 0.8 %copy-done.4 = f32[3,35,35]{2,1,0:T(8,128)S(1)} copy-done((f32[3,35,35]{2,1,0:T(8,128)S(1)}, f32[3,35,35]{2,1,0:T(8,128)}, u32[]{:S(2)}) %copy-start.4) | copy-done | bytes 14724
  5.2 0.0 copy-start.8
  5.2 0.7 %copy-done.8 = s32[1,2,5,2]{2,3,1,0:T(2,128)S(1)} copy-done((s32[1,2,5,2]{2,3,1,0:T(2,128)S(1)}, s32[1,2,5,2]{2,3,1,0:T(2,128)}, u32[]{:S(2)}) %copy-start.8) | copy-done | bytes 104
  5.9 0.0 copy-start.11
  5.9 0.7 %copy-done.11 = s32[128]{0:T(128)S(1)} copy-done((s32[128]{0:T(128)S(1)}, s32[128]{0:T(128)}, u32[]{:S(2)}) %copy-start.11) | copy-done | bytes 536
  6.5 18.7 %shard_map.118 = f32[9,35,128]{2,1,0:T(8,128)S(1)} custom-call(f32[9,35,128]{2,1,0:T(8,128)S(1)} %bitcast.11, f32[9,9,3,128]{3,2,1,0:T(4,128)S(1)} %bitcast.12, f32[3,4,128]{2,1,0:T(4,128)S(1)} %copy-done.6, f32[1,128]{1,0:T(1,128)S(1)} %bitcast.17, f32[1,128]{1,0:T(1,128)S(1)} %bitcast.18, f32[3,35,35]{2,1,0:T(8,128)S(1)} %copy-done.4, ...), custom_call_target="tpu_custom_call" | custom-call | tf_op jit(solution)/shard_map/pallas_call | solution.py:315
  25.2 0.7 %copy.14 = f32[35,9,128]{2,0,1:T(8,128)} copy(f32[35,9,128]{2,0,1:T(8,128)S(1)} %bitcast.10) | data formatting | bytes 322560
Async XLA Ops:
  0.0 0.7 %copy-start.7 = (s32[4,128]{1,0:T(4,128)S(1)}, s32[4,128]{1,0:T(4,128)}, u32[]{:S(2)}) copy-start(s32[4,128]{1,0:T(4,128)} %face_source.1) | copy-start | bytes 6148
  0.0 0.7 %copy-start.5 = (s32[1,2,5,2,4]{2,4,3,1,0:T(4,128)S(1)}, s32[1,2,5,2,4]{2,4,3,1,0:T(4,128)}, u32[]{:S(2)}) copy-start(s32[1,2,5,2,4]{2,4,3,1,0:T(4,128)} %param.22) | copy-start | bytes 964
  0.0 0.7 %copy-start.6 = (f32[3,4,128]{2,1,0:T(4,128)S(1)}, f32[3,4,128]{2,1,0:T(4,128)}, u32[]{:S(2)}) copy-start(f32[3,4,128]{2,1,0:T(4,128)} %normals.1) | copy-start | bytes 18436
  0.0 0.7 %copy-start.9 = (f32[128]{0:T(128)S(1)}, f32[128]{0:T(128)}, u32[]{:S(2)}) copy-start(f32[128]{0:T(128)} %param.15) | copy-start | bytes 1540
  0.0 0.7 %copy-start.10 = (f32[128]{0:T(128)S(1)}, f32[128]{0:T(128)}, u32[]{:S(2)}) copy-start(f32[128]{0:T(128)} %param.16) | copy-start | bytes 1540
  0.7 0.9 %copy-start = (f32[35,9,128]{2,0,1:T(8,128)S(1)}, f32[35,9,128]{2,0,1:T(8,128)}, u32[]{:S(2)}) copy-start(f32[35,9,128]{2,0,1:T(8,128)} %param.12) | copy-start | bytes 483844
  1.7 0.9 %copy-start.1 = (f32[3,9,9,128]{3,0,2,1:T(4,128)S(1)}, f32[3,9,9,128]{3,0,2,1:T(4,128)}, u32[]{:S(2)}) copy-start(f32[3,9,9,128]{3,0,2,1:T(4,128)} %param.13) | copy-start | bytes 373252
  2.6 0.9 %copy-start.2 = (f32[4,35,35]{2,0,1:T(4,128)S(1)}, f32[4,35,35]{2,0,1:T(4,128)}, u32[]{:S(2)}) copy-start(f32[4,35,35]{2,0,1:T(4,128)} %param.18) | copy-start | bytes 58804
  3.5 0.9 %copy-start.3 = (f32[4,35,35]{2,0,1:T(4,128)S(1)}, f32[4,35,35]{2,0,1:T(4,128)}, u32[]{:S(2)}) copy-start(f32[4,35,35]{2,0,1:T(4,128)} %param.19) | copy-start | bytes 58804
  4.3 0.8 %copy-start.4 = (f32[3,35,35]{2,1,0:T(8,128)S(1)}, f32[3,35,35]{2,1,0:T(8,128)}, u32[]{:S(2)}) copy-start(f32[3,35,35]{2,1,0:T(8,128)} %stiffness.1) | copy-start | bytes 44104
  5.2 0.7 %copy-start.8 = (s32[1,2,5,2]{2,3,1,0:T(2,128)S(1)}, s32[1,2,5,2]{2,3,1,0:T(2,128)}, u32[]{:S(2)}) copy-start(s32[1,2,5,2]{2,3,1,0:T(2,128)} %param.23) | copy-start | bytes 244
  5.9 0.7 %copy-start.11 = (s32[128]{0:T(128)S(1)}, s32[128]{0:T(128)}, u32[]{:S(2)}) copy-start(s32[128]{0:T(128)} %param.20) | copy-start | bytes 1540
where the time goes:
time: 26.2 us; the launch traced here: 25.9 us
  Pallas kernels  18.7 us (71%)
  local copies, waits for them, and re-layouts  7.17 us (27%)
    pallas_call x1, Pallas kernels, per_device(): pl.pallas_call(functools.partial(kernel, n_dom, n_sub), out_shape=jax.Sha...  18.7 us
    unnamed x25, local copies, waits for them, and re-layouts  7.17 us

commit v1 on v0

--- a/solution.py
+++ b/solution.py
@@ -39,39 +39,18 @@
 def kernel(
     n_dom,
     n_sub,
-    modal,
-    star,
-    normals,
-    speed,
-    jacobian,
-    stiffness,
-    lift_minus,
-    lift_plus,
-    cluster,
-    face_source,
-    send_rows,
-    send_counts,
-    out,
-    grad_mat,
-    back_mat,
-    lift_mat,
-    cur,
-    early,
-    late,
-    mid,
-    value,
-    coarse,
-    zed,
-    dee,
-    faces,
-    slot_rows,
-    near_hot,
-    far_hot,
-    send_buf,
-    recv_buf,
-    send_sem,
-    recv_sem,
+    *refs,
 ):
+    count = 12
+    sources, held = refs[:count], refs[-count:]
+    (
+        out, grad_mat, back_mat, lift_mat, far_mat, cur, early, late, mid, value, coarse,
+        zed, dee, faces, slot_rows, near_hot, far_hot, send_buf, recv_buf, send_sem, recv_sem, load_sem,
+    ) = refs[count:-count]
+    (
+        modal, star, normals, speed, jacobian, stiffness,
+        lift_minus, lift_plus, cluster, face_source, send_rows, send_counts,
+    ) = held
     quants, basis, elems = modal.shape
     rows = cur.shape[0]
     offsets = send_counts.shape[3]
@@ -96,6 +75,15 @@
                 def _():
                     action(o, t, other)
 
+    def load(index):
+        return pltpu.make_async_copy(sources[index], held[index], load_sem.at[index])
+
+    def wait_for(*wanted):
+        for ref in wanted:
+            load([ref is other for other in held].index(True)).wait()
+
+    for index in (10, 11, 5, 0, 1, 2, 3, 4, 6, 7, 8, 9):
+        load(index).start()
     barrier = pltpu.get_barrier_semaphore()
     recv_buf[...] = jnp.zeros_like(recv_buf)
 
@@ -104,39 +92,7 @@
 
     partners(1, greet)
 
-    for scratch in (grad_mat, back_mat, lift_mat, cur):
-        scratch[...] = jnp.zeros_like(scratch)
-
-    def place(ref, row, column, matrix):
-        high, low = halves(matrix)
-        for index, part in enumerate((high, low, high)):
-            start = column + index * rows
-            ref[row : row + basis, start : start + basis] = part
-
-    for d in range(3):
-        place(grad_mat, d * rows, 0, -stiffness[d])
-        place(back_mat, d * rows, 0, stiffness[d].T)
-    for f in range(4):
-        own, far = 0.5 * lift_minus[:, f, :], 0.5 * lift_plus[:, f, :]
-        place(lift_mat.at[f], 0, 0, own)
-        place(lift_mat.at[f], 0, 3 * rows, far)
-        place(lift_mat.at[f], rows, 0, own)
-        place(lift_mat.at[f], rows, 3 * rows, -far)
-
-    for q in range(quants):
-        cur[:basis, lane(q)] = modal[q]
-
-    coarse_row = cluster[...]
-    is_fine = coarse_row == 0
-    near_iota = lax.broadcasted_iota(jnp.int32, (elems, elems), 0)
-    far_iota = lax.broadcasted_iota(jnp.int32, (pool_rows, elems), 0)
-    for f in range(4):
-        source = face_source[f : f + 1, :]
-        near_hot[:, lane(f)] = jnp.where(near_iota == source, 1.0, 0.0)
-        index = source - elems
-        block = index // slots
-        index = jnp.where(index >= 0, block * (2 * slots) + (index - block * slots) + slots * coarse_row, -1)
-        far_hot[:, lane(f)] = jnp.where(far_iota == index, 1.0, 0.0)
+    wait_for(send_rows, send_counts)
     slot_iota = lax.broadcasted_iota(jnp.int32, (slots, elems), 0)
     for o in range(offsets):
         for t in range(n_sub):
@@ -148,6 +104,46 @@
     send_iota = lax.broadcasted_iota(jnp.int32, (pool_rows, elems), 1)
     send_hot = jnp.where(send_iota == slot_rows[...], 1.0, 0.0)
     slot_list = (lax.broadcasted_iota(jnp.int32, (pool_rows, elems), 0) // slots) % 2
+
+    def place(ref, row, column, matrix):
+        high, low = halves(matrix)
+        for index, part in enumerate((high, low, high)):
+            start = column + index * rows
+            ref[row : row + basis, start : start + basis] = part
+
+    grad_mat[...] = jnp.zeros_like(grad_mat)
+    wait_for(stiffness)
+    for d in range(3):
+        place(grad_mat, d * rows, 0, -stiffness[d])
+    cur[...] = jnp.zeros_like(cur)
+    wait_for(modal)
+    for q in range(quants):
+        cur[:basis, lane(q)] = modal[q]
+
+    def prepare():
+        wait_for(normals, speed, jacobian, lift_minus, lift_plus, cluster, face_source)
+        for scratch in (back_mat, lift_mat, far_mat):
+            scratch[...] = jnp.zeros_like(scratch)
+        for d in range(3):
+            place(back_mat, d * rows, 0, stiffness[d].T)
+        for f in range(4):
+            own, far = 0.5 * lift_minus[:, f, :], 0.5 * lift_plus[:, f, :]
+            place(lift_mat.at[f], 0, 0, own)
+            place(lift_mat.at[f], 0, 3 * rows, far)
+            place(lift_mat.at[f], rows, 0, own)
+            place(lift_mat.at[f], rows, 3 * rows, -far)
+            place(far_mat.at[f], 0, 0, far)
+        coarse_row = cluster[...]
+        near_iota = lax.broadcasted_iota(jnp.int32, (elems, elems), 0)
+        far_iota = lax.broadcasted_iota(jnp.int32, (pool_rows, elems), 0)
+        for f in range(4):
+            source = face_source[f : f + 1, :]
+            near_hot[:, lane(f)] = jnp.where(near_iota == source, 1.0, 0.0)
+            index = source - elems
+            block = index // slots
+            spot = block * (2 * slots) + (index - block * slots) + slots * coarse_row
+            index = jnp.where(index >= 0, spot, -1)
+            far_hot[:, lane(f)] = jnp.where(far_iota == index, 1.0, 0.0)
 
     def stacked(source):
         high, low = halves(source)
@@ -228,47 +224,56 @@
         high, low = halves(source)
         return matmul(hot, high, ((1,), (1,))) + matmul(hot, low, ((1,), (1,)))
 
+    wide = quants * rows
+
+    def gathered(left, right):
+        high, low = halves(left)
+        faces[...] = matmul(jnp.concatenate([high, low], axis=0), right)
+
+    def face_values(f):
+        parts = [
+            jnp.concatenate(
+                [faces[base + q * rows : base + (q + 1) * rows, lane(f)] for q in range(quants)],
+                axis=1,
+            )
+            for base in (0, wide)
+        ]
+        return jnp.concatenate([parts[0], parts[0], parts[1]], axis=0).astype(bf16)
+
+    def spread(lifted):
+        for q in range(quants):
+            for d in range(3):
+                total = zed[d * rows : (d + 1) * rows, lane(q)]
+                for f in range(4):
+                    total = total - normals[d, f : f + 1, :] * lifted[f][:rows, lane(q)]
+                zed[d * rows : (d + 1) * rows, lane(q)] = total
+
     def update(turn, integral, near_left, near_right, finish):
-        high, low = halves(near_left)
-        faces[...] = matmul(jnp.concatenate([high, low], axis=0), near_right)
+        gathered(near_left, near_right)
         own = stacked(integral)
         zed[...] = matmul(back_mat[...], own)
+        lifted = [
+            matmul(lift_mat[f], jnp.concatenate([own, face_values(f)], axis=0)) for f in range(4)
+        ]
+        spread(lifted)
+        dee[...] = (lifted[0][rows:] + lifted[1][rows:]) + (lifted[2][rows:] + lifted[3][rows:])
         partners(-1, lambda o, t, other: arrival(turn, o, t, other).wait_recv())
         pool = recv_buf[turn].reshape(pool_rows, recv_buf.shape[3])
-        high, low = halves(pool.T)
-        wide = quants * rows
-        faces[...] += matmul(jnp.concatenate([high[:wide], low[:wide]], axis=0), far_hot[...])
-        for f in range(4):
-            parts = [
-                jnp.concatenate(
-                    [
-                        faces[base + q * rows : base + (q + 1) * rows, lane(f)]
-                        for q in range(quants)
-                    ],
-                    axis=1,
-                )
-                for base in (0, wide)
-            ]
-            theirs = jnp.concatenate([parts[0], parts[0], parts[1]], axis=0).astype(bf16)
-            lifted = matmul(lift_mat[f, :, : 3 * rows], own) + matmul(
-                lift_mat[f, :, 3 * rows :], theirs
-            )
-            for q in range(quants):
-                block = lifted[:rows, lane(q)]
-                for d in range(3):
-                    zed[d * rows : (d + 1) * rows, lane(q)] -= (
-                        normals[d, f : f + 1, :] * block
-                    )
-                other = lifted[rows:, lane(q)]
-                dee[:, lane(q)] = other if f == 0 else dee[:, lane(q)] + other
+        gathered(pool.T[:wide], far_hot[...])
+        lifted = [matmul(far_mat[f], face_values(f)) for f in range(4)]
+        spread(lifted)
+        dee[...] -= (lifted[0] + lifted[1]) + (lifted[2] + lifted[3])
         mix(lambda q, total: finish(q, total - speed[...] * dee[:, lane(q)]))
 
     early[...] = HALF * cur[...]
     late[...] = HALF * cur[...]
     mid[...] = cur[...]
+    wait_for(star)
     expand([(early, weights(0.0, HALF)), (late, weights(HALF, 2 * HALF))])
     early_tall = tall(early[...])
     send(0, pick(send_hot, early_tall))
+    prepare()
+    is_fine = cluster[...] == 0
 
     def keep_mid(q, total):
         result = mid[:, lane(q)] + jacobian[...] * total
@@ -312,36 +317,7 @@
     pool_rows = blocks * 2 * slots
     message = (2, blocks, 2 * slots, up(quants * rows, 128))
     state = pltpu.VMEM((rows, wide), f32)
-    result = pl.pallas_call(
-        functools.partial(kernel, n_dom, n_sub),
-        out_shape=jax.ShapeDtypeStruct((quants, basis, elems), f32),
-        in_specs=[pl.BlockSpec(memory_space=pltpu.VMEM)] * 12,
-        out_specs=pl.BlockSpec(memory_space=pltpu.VMEM),
-        scratch_shapes=[
-            pltpu.VMEM((3 * rows, 3 * rows), f32),
-            pltpu.VMEM((3 * rows, 3 * rows), f32),
-            pltpu.VMEM((4, 2 * rows, 6 * rows), f32),
-            state,
-            state,
-            state,
-            state,
-            state,
-            state,
-            pltpu.VMEM((3 * rows, wide), f32),
-            state,
-            pltpu.VMEM((2 * quants * rows, 4 * elems), f32),
-            pltpu.VMEM((pool_rows, elems), jnp.int32),
-            pltpu.VMEM((elems, 4 * elems), f32),
-            pltpu.VMEM((pool_rows, 4 * elems), f32),
-            pltpu.VMEM(message, f32),
-            pltpu.VMEM(message, f32),
-            pltpu.SemaphoreType.DMA((2, blocks)),
-            pltpu.SemaphoreType.DMA((2, blocks)),
-        ],
-        compiler_params=pltpu.CompilerParams(
-            collective_id=0, has_side_effects=True, vmem_limit_bytes=32 * 1024 * 1024
-        ),
-    )(
+    operands = (
         modal_state.transpose(1, 0, 2),
         star_matrices.transpose(1, 2, 0, 3),
         face_normals,
@@ -355,6 +331,39 @@
         send_rows.transpose(0, 1, 3, 4, 2),
         send_counts.transpose(0, 1, 3, 2),
     )
+    result = pl.pallas_call(
+        functools.partial(kernel, n_dom, n_sub),
+        out_shape=jax.ShapeDtypeStruct((quants, basis, elems), f32),
+        in_specs=[pl.BlockSpec(memory_space=pltpu.HBM)] * len(operands),
+        out_specs=pl.BlockSpec(memory_space=pltpu.VMEM),
+        scratch_shapes=[
+            pltpu.VMEM((3 * rows, 3 * rows), f32),
+            pltpu.VMEM((3 * rows, 3 * rows), f32),
+            pltpu.VMEM((4, 2 * rows, 6 * rows), f32),
+            pltpu.VMEM((4, rows, 3 * rows), f32),
+            state,
+            state,
+            state,
+            state,
+            state,
+            state,
+            pltpu.VMEM((3 * rows, wide), f32),
+            state,
+            pltpu.VMEM((2 * quants * rows, 4 * elems), f32),
+            pltpu.VMEM((pool_rows, elems), jnp.int32),
+            pltpu.VMEM((elems, 4 * elems), f32),
+            pltpu.VMEM((pool_rows, 4 * elems), f32),
+            pltpu.VMEM(message, f32),
+            pltpu.VMEM(message, f32),
+            pltpu.SemaphoreType.DMA((2, blocks)),
+            pltpu.SemaphoreType.DMA((2, blocks)),
+            pltpu.SemaphoreType.DMA((len(operands),)),
+        ]
+        + [pltpu.VMEM(operand.shape, operand.dtype) for operand in operands],
+        compiler_params=pltpu.CompilerParams(
+            collective_id=0, has_side_effects=True, vmem_limit_bytes=60 * 1024 * 1024
+        ),
+    )(*operands)
     return result.transpose(1, 0, 2)
 
 

time: 26.2 us -> 20.9 us (0.80)
  local copies, waits for them, and re-layouts: 7.17 us -> 1.61 us
  Pallas kernels: 18.7 us -> 19.1 us
    unnamed x25 -> x1, local copies, waits for them, and re-layouts: 7.17 us -> 1.61 us
    pallas_call x1, Pallas kernels: 18.7 us -> 19.1 us  [per_device(): pl.pallas_call(functools.partial(kernel, n_dom, n_sub), out_shape=jax.Sha...]
where the time goes in v1:
time: 20.9 us; the launch traced here: 20.7 us
  Pallas kernels  19.1 us (91%)
  local copies, waits for them, and re-layouts  1.61 us (8%)
    pallas_call x1, Pallas kernels, per_device(): pl.pallas_call(functools.partial(kernel, n_dom, n_sub), out_shape=jax.Sha...  19.1 us
    unnamed x1, local copies, waits for them, and re-layouts  1.61 us

profile of v1, /device:TPU:0, one launch (start us, length us, event | category | flops | bytes accessed | tf_op | source)
XLA Modules:
  0.0 20.7 jit_solution(8043432901603917600)
XLA Ops:
  0.0 19.1 %shard_map.118 = f32[9,35,128]{2,1,0:T(8,128)} custom-call(f32[9,35,128]{2,1,0:T(8,128)} %bitcast.11, f32[9,9,3,128]{3,2,1,0:T(4,128)} %bitcast.12, f32[3,4,128]{2,1,0:T(4,128)} %refs_2_.1, f32[1,128]{1,0:T(1,128)} %bitcast.17, f32[1,128]{1,0:T(1,128)} %bitcast.18, f32[3,35,35]{2,1,0:T(8,128)} %refs_5_.1, f32[35,4,35]{2,1,0:T(4,128)} %bitcast.13, ...), custom_call_target="tpu_custom_call" | custom-call | tf_op jit(solution)/shard_map/pallas_call | solution.py:334
  19.1 1.6 %copy.14 = f32[35,9,128]{2,0,1:T(8,128)} copy(f32[35,9,128]{2,0,1:T(8,128)} %bitcast.10) | data formatting | bytes 322560

commit v2 on v1

--- a/solution.py
+++ b/solution.py
@@ -44,7 +44,7 @@
     count = 12
     sources, held = refs[:count], refs[-count:]
     (
-        out, grad_mat, back_mat, lift_mat, far_mat, cur, early, late, mid, value, coarse,
+        out, grad_mat, back_mat, lift_mat, far_mat, cur, fresh, early, late, mid, value, coarse,
         zed, dee, faces, slot_rows, near_hot, far_hot, send_buf, recv_buf, send_sem, recv_sem, load_sem,
     ) = refs[count:-count]
     (
@@ -114,7 +114,10 @@
     grad_mat[...] = jnp.zeros_like(grad_mat)
     wait_for(stiffness)
     for d in range(3):
-        place(grad_mat, d * rows, 0, -stiffness[d])
+        high, low = halves(-stiffness[d])
+        for row, start, part in ((0, 0, high), (0, 3 * rows, high), (rows, 0, low)):
+            start += d * rows
+            grad_mat[row : row + basis, start : start + basis] = part
     cur[...] = jnp.zeros_like(cur)
     wait_for(modal)
     for q in range(quants):
@@ -168,15 +171,27 @@
 
     def expand(sums):
         def step(index, carry):
-            zed[...] = matmul(grad_mat[...], stacked(cur[...]))
             scales = [pick_coefficient(index, values) for _, values in sums]
-
-            def finish(q, total):
-                cur[:, lane(q)] = total
-                for (ref, _), scale in zip(sums, scales):
-                    ref[:, lane(q)] = ref[:, lane(q)] + scale * total
-
-            mix(finish)
+            for first in range(0, quants, 2):
+                wanted = range(first, min(first + 2, quants))
+                mixed = []
+                for q in wanted:
+                    totals = [None] * 3
+                    for p in range(quants):
+                        block = cur[:, lane(p)]
+                        for d in range(3):
+                            term = block * star[p, q, d : d + 1, :]
+                            totals[d] = term if totals[d] is None else totals[d] + term
+                    high, low = halves(jnp.concatenate(totals, axis=0))
+                    mixed.append(jnp.concatenate([high, low], axis=0).astype(bf16))
+                product = matmul(grad_mat[...], jnp.concatenate(mixed, axis=1))
+                product = product[:rows] + product[rows:]
+                for q in wanted:
+                    total = product[:, lane(q - first)]
+                    fresh[:, lane(q)] = total
+                    for (ref, _), scale in zip(sums, scales):
+                        ref[:, lane(q)] = ref[:, lane(q)] + scale * total
+            cur[...] = fresh[...]
             return carry
 
         lax.fori_loop(0, DEGREE, step, 0)
@@ -276,10 +291,11 @@
     is_fine = cluster[...] == 0
 
     def keep_mid(q, total):
-        result = mid[:, lane(q)] + jacobian[...] * total
+        change = jacobian[...] * total
+        result = mid[:, lane(q)] + change
         cur[:, lane(q)] = result
         value[:, lane(q)] = HALF * result
-        mid[:, lane(q)] = jnp.where(is_fine, result, mid[:, lane(q)])
+        mid[:, lane(q)] = jnp.where(is_fine, change, 0.0)
 
     update(0, early[...], early_tall, near_hot[...], keep_mid)
     expand([(value, weights(0.0, HALF))])
@@ -337,10 +353,11 @@
         in_specs=[pl.BlockSpec(memory_space=pltpu.HBM)] * len(operands),
         out_specs=pl.BlockSpec(memory_space=pltpu.VMEM),
         scratch_shapes=[
-            pltpu.VMEM((3 * rows, 3 * rows), f32),
+            pltpu.VMEM((2 * rows, 6 * rows), f32),
             pltpu.VMEM((3 * rows, 3 * rows), f32),
             pltpu.VMEM((4, 2 * rows, 6 * rows), f32),
             pltpu.VMEM((4, rows, 3 * rows), f32),
+            state,
             state,
             state,
             state,
@@ -364,7 +381,7 @@
             collective_id=0, has_side_effects=True, vmem_limit_bytes=60 * 1024 * 1024
         ),
     )(*operands)
-    return result.transpose(1, 0, 2)
+    return modal_state + result.transpose(1, 0, 2)
 
 
 def solution(mesh):

time: 20.9 us -> 20.5 us (0.981)
  other arithmetic: 0 us -> 1.62 us
  local copies, waits for them, and re-layouts: 1.61 us -> 0.01 us
  Pallas kernels: 19.1 us -> 18.7 us
    add x0 -> x1, other arithmetic: none -> 1.62 us  [per_device(): return modal_state + result.transpose(1, 0, 2)]
    unnamed x1 -> x2, local copies, waits for them, and re-layouts: 1.61 us -> 0.01 us
    pallas_call x1, Pallas kernels: 19.1 us -> 18.7 us  [per_device(): pl.pallas_call(functools.partial(kernel, n_dom, n_sub), out_shape=jax.Sha...]
where the time goes in v2:
time: 20.5 us; the launch traced here: 20.4 us
  Pallas kernels  18.7 us (91%)
  other arithmetic  1.62 us (8%)
    pallas_call x1, Pallas kernels, per_device(): pl.pallas_call(functools.partial(kernel, n_dom, n_sub), out_shape=jax.Sha...  18.7 us
    add x1, other arithmetic, per_device(): return modal_state + result.transpose(1, 0, 2)  1.62 us

profile of v2, /device:TPU:0, one launch (start us, length us, event | category | flops | bytes accessed | tf_op | source)
XLA Modules:
  0.0 20.4 jit_solution(3371654069077735637)
XLA Ops:
  0.0 0.0 copy-start
  0.0 18.7 %shard_map.118 = f32[9,35,128]{2,1,0:T(8,128)} custom-call(f32[9,35,128]{2,1,0:T(8,128)} %bitcast.11, f32[9,9,3,128]{3,2,1,0:T(4,128)} %bitcast.12, f32[3,4,128]{2,1,0:T(4,128)} %refs_2_.1, f32[1,128]{1,0:T(1,128)} %bitcast.17, f32[1,128]{1,0:T(1,128)} %bitcast.18, f32[3,35,35]{2,1,0:T(8,128)} %refs_5_.1, f32[35,4,35]{2,1,0:T(4,128)} %bitcast.13, ...), custom_call_target="tpu_custom_call" | custom-call | tf_op jit(solution)/shard_map/pallas_call | solution.py:350
  18.7 0.0 copy-done
  18.7 1.6 %bitcast_add_fusion = f32[35,9,128]{2,0,1:T(8,128)} fusion(f32[35,9,128]{2,0,1:T(8,128)S(1)} %copy-done, f32[9,35,128]{2,1,0:T(8,128)} %shard_map.118), kind=kLoop, calls=%fused_computation | loop fusion | flops 40320 | bytes 483840 | tf_op jit(solution)/shard_map/add | solution.py:384
Async XLA Ops:
  0.0 18.7 %copy-start = (f32[35,9,128]{2,0,1:T(8,128)S(1)}, f32[35,9,128]{2,0,1:T(8,128)}, u32[]{:S(2)}) copy-start(f32[35,9,128]{2,0,1:T(8,128)} %param.12) | copy-start | bytes 483844

commit v3 on v2

--- a/solution.py
+++ b/solution.py
@@ -316,7 +316,7 @@
         cur[:, lane(q)] = jnp.where(is_fine, value[:, lane(q)], coarse[:, lane(q)])
 
     def keep_end(q, total):
-        out[q] = (mid[:, lane(q)] + jacobian[...] * total)[:basis]
+        out[q] = modal[q] + (mid[:, lane(q)] + jacobian[...] * total)[:basis]
 
     update(1, cur[...], both, near_both, keep_end)
     for turn in range(2):
@@ -349,7 +349,7 @@
     )
     result = pl.pallas_call(
         functools.partial(kernel, n_dom, n_sub),
-        out_shape=jax.ShapeDtypeStruct((quants, basis, elems), f32),
+        out_shape=pltpu.VMEM((quants, basis, elems), f32),
         in_specs=[pl.BlockSpec(memory_space=pltpu.HBM)] * len(operands),
         out_specs=pl.BlockSpec(memory_space=pltpu.VMEM),
         scratch_shapes=[
@@ -381,7 +381,7 @@
             collective_id=0, has_side_effects=True, vmem_limit_bytes=60 * 1024 * 1024
         ),
     )(*operands)
-    return modal_state + result.transpose(1, 0, 2)
+    return result.transpose(1, 0, 2)
 
 
 def solution(mesh):

time: 20.5 us -> 18.9 us (0.922)
  other arithmetic: 1.62 us -> 0 us
  Pallas kernels: 18.7 us -> 18 us
  local copies, waits for them, and re-layouts: 0.01 us -> 0.68 us
    add x1 -> x0, other arithmetic: 1.62 us -> none  [per_device(): return modal_state + result.transpose(1, 0, 2)]
    pallas_call x1, Pallas kernels: 18.7 us -> 18 us  [per_device(): pl.pallas_call(functools.partial(kernel, n_dom, n_sub), out_shape=pltpu.V...]
    unnamed x2 -> x1, local copies, waits for them, and re-layouts: 0.01 us -> 0.68 us
where the time goes in v3:
time: 18.9 us; the launch traced here: 18.7 us
  Pallas kernels  18 us (95%)
  local copies, waits for them, and re-layouts  0.68 us (4%)
    pallas_call x1, Pallas kernels, per_device(): pl.pallas_call(functools.partial(kernel, n_dom, n_sub), out_shape=pltpu.V...  18 us
    unnamed x1, local copies, waits for them, and re-layouts  0.68 us

profile of v3, /device:TPU:0, one launch (start us, length us, event | category | flops | bytes accessed | tf_op | source)
XLA Modules:
  0.0 18.7 jit_solution(7878466118606403876)
XLA Ops:
  0.0 18.0 %shard_map.118 = f32[9,35,128]{2,1,0:T(8,128)S(1)} custom-call(f32[9,35,128]{2,1,0:T(8,128)} %bitcast.11, f32[9,9,3,128]{3,2,1,0:T(4,128)} %bitcast.12, f32[3,4,128]{2,1,0:T(4,128)} %refs_2_.1, f32[1,128]{1,0:T(1,128)} %bitcast.17, f32[1,128]{1,0:T(1,128)} %bitcast.18, f32[3,35,35]{2,1,0:T(8,128)} %refs_5_.1, f32[35,4,35]{2,1,0:T(4,128)} %bitcast.13, ...), custom_call_target="tpu_custom_call" | custom-call | tf_op jit(solution)/shard_map/pallas_call | solution.py:350
  18.1 0.7 %copy.14 = f32[35,9,128]{2,0,1:T(8,128)} copy(f32[35,9,128]{2,0,1:T(8,128)S(1)} %bitcast.10) | data formatting | bytes 322560
